TPU v7x, 32 devices: a whole 2x2x4 slice. The times are simulated.
32 devices in a mesh: wide: 8 (over y, x, core), grp: 4 (over z).
Axes of the slice: x: 2, y: 2, z: 4, core: 2. Of those that a mesh axis runs over, the one named last changes fastest.
Arguments:
- embeds: bfloat16 [9216, 1024], P(('wide', 'grp')), may hold values from -700 to 700
- bucket: int32 [9216], P(('wide', 'grp')), may hold values from 0 to 7, as said below
- pairs: int32 [128], P(('wide', 'grp')), may hold values from -1 to 3, as said below
Outputs:
- density: float32 [32, 384], P(('wide', 'grp'))
Inputs may be any that keep to these rules, and one draw needn't show every extreme that they name: At most 48 rows of one file shard name the same bucket; for every g some bucket is named by exactly 48 rows of every shard (s, g). `pairs`: the 4 entries of block (o, g) name distinct blocks (o, b) by b, live entries first and -1 after; for every o some block has all 4 entries live.
All inputs are finite; a program needn't handle non-finite values.
Results may differ from a plain program's by a relative error of at most 0.0034.
Values may be sent and summed in bfloat16 or wider, within the bound.
A program may use at most 64 MiB of HBM per device.

v0:
```python
import jax
import jax.numpy as jnp
from jax import lax
from jax.sharding import PartitionSpec as P

BLK = 384


SHARPNESS = 10.0
EPSILON = 1e-06


def pair_sums(left_rows, right_rows, right_weight):
    cosines = lax.dot_general(
        left_rows, right_rows, (((1,), (1,)), ((), ())), preferred_element_type=jnp.float32
    )
    return jnp.sum(jnp.exp(SHARPNESS * (cosines - 1.0)) * right_weight[None, :], axis=1)


def per_device(embeds, bucket, pairs):
    wide_count = lax.axis_size("wide")
    feature_width = embeds.shape[1]
    capacity = BLK // wide_count
    floats = embeds.astype(jnp.float32)
    unit_rows = (
        floats * lax.rsqrt(jnp.sum(floats * floats, axis=1, keepdims=True) + EPSILON)
    ).astype(jnp.bfloat16)
    onehot = (bucket[:, None] == jnp.arange(wide_count, dtype=jnp.int32)[None, :]).astype(jnp.int32)
    row_ranks = jnp.sum(jnp.cumsum(onehot, axis=0) * onehot, axis=1) - 1
    counts = jnp.sum(onehot, axis=0)
    send_slots = bucket * capacity + row_ranks
    outgoing = (
        jnp.zeros((wide_count * capacity, feature_width), jnp.bfloat16)
        .at[send_slots]
        .set(unit_rows)
    )
    received, arrived = (
        lax.all_to_all(
            outgoing.reshape(wide_count, capacity, feature_width),
            "wide",
            split_axis=0,
            concat_axis=0,
            tiled=True,
        ),
        lax.all_to_all(
            counts.reshape(wide_count, 1), "wide", split_axis=0, concat_axis=0, tiled=True
        ),
    )
    arrived = arrived.reshape(wide_count)
    offsets = jnp.cumsum(arrived) - arrived
    within = jnp.arange(capacity, dtype=jnp.int32)
    places = jnp.where(within[None, :] < arrived[:, None], offsets[:, None] + within[None, :], BLK)
    own_block = (
        jnp.zeros((BLK, feature_width), jnp.bfloat16)
        .at[places.reshape(-1)]
        .set(received.reshape(wide_count * capacity, feature_width), mode="drop")
    )
    total_rows = jnp.sum(arrived)
    valid_rows = (jnp.arange(BLK, dtype=jnp.int32) < total_rows).astype(jnp.float32)
    flags_wire = valid_rows.astype(jnp.bfloat16)
    live_count = jnp.sum((pairs >= 0).astype(jnp.int32))
    first_row = jnp.int32(0)
    panel_rows = lax.all_gather(own_block, "grp", axis=0, tiled=True)
    panel_flags = lax.all_gather(flags_wire, "grp", axis=0, tiled=True)
    length = panel_rows.shape[0]
    span_rows = min(BLK, length)

    def add_pair(pair_index, running_sum):
        target = pairs[pair_index] * BLK
        shift_rows = jnp.clip(target, 0, length - span_rows)

        def add_tile(before):
            right_rows = lax.dynamic_slice_in_dim(panel_rows, shift_rows, span_rows, 0)
            right_flags = lax.dynamic_slice_in_dim(panel_flags, shift_rows, span_rows, 0).astype(
                jnp.float32
            )
            global_rows = shift_rows + jnp.arange(span_rows, dtype=jnp.int32)
            inside = (global_rows >= target) & (global_rows < target + BLK)
            return before + pair_sums(own_block, right_rows, jnp.where(inside, right_flags, 0.0))

        touches = (target < first_row + length) & (target + BLK > first_row)
        return lax.cond(touches, add_tile, lambda before: before, running_sum)

    density = lax.fori_loop(0, live_count, add_pair, jnp.zeros((BLK,), jnp.float32))
    return (density * valid_rows).reshape(1, BLK)


def solution(mesh):
    placed = (P(("wide", "grp"), None), P(("wide", "grp")), P(("wide", "grp")))
    return jax.shard_map(
        per_device, mesh=mesh, in_specs=placed, out_specs=P(("wide", "grp"), None), check_vma=False
    )
```

profile of v0, /device:TPU:0, one launch (start us, length us, event | category | flops | bytes accessed | tf_op | source)
XLA Modules:
  0.0 128.0 jit_solution(16855118370291000521)
XLA Ops:
  6.5 0.7 iota_compare_fusion
  7.2 0.9 reduce-window.19
  8.1 0.2 slice_reduce_fusion
  8.4 0.8 fusion.17
  9.2 0.7 copy.5
  9.9 5.2 %all-to-all-start = ((s32[8,1,1]{2,1,0:T(1,128)}), s32[8,1,1]{2,1,0:T(1,128)S(1)}, u32[]{:S(2)}, u32[]{:S(2)}) async-start(s32[8,1,1]{2,1,0:T(1,128)} %copy.5), calls=%async_computation | async-start | bytes 8192 | tf_op jit(solution)/shard_map/all_to_all | solution.py:45
  15.1 1.3 fusion.9
  16.4 0.7 compare_select_fusion.1
  17.1 3.3 %scatter_custom_fusion = bf16[384,1024]{1,0:T(8,128)(2,1)} fusion(s32[288]{0:T(512)S(1)} %compare_select_fusion.1, bf16[288,1024]{1,0:T(8,128)(2,1)} %param.7, f32[288]{0:T(512)S(1)} %add_rsqrt_fusion, bf16[]{:T(256)} %constant.61.clone.1), kind=kCustom, calls=%fused_computation.18 | custom fusion | flops 884736 | bytes 1378306 | tf_op jit(solution)/shard_map/scatter | solution.py:35
  20.4 4.2 %all-to-all-start.1 = ((bf16[8,48,1024]{2,1,0:T(8,128)(2,1)}), bf16[8,48,1024]{2,1,0:T(8,128)(2,1)S(1)}, u32[]{:S(2)}, u32[]{:S(2)}) async-start(bf16[8,48,1024]{2,1,0:T(8,128)(2,1)} %bitcast.6), calls=%async_computation.1 | async-start | bytes 1572864 | tf_op jit(solution)/shard_map/all_to_all | solution.py:38
  24.6 0.8 fusion.21
  25.8 11.4 %all-to-all-done.1 = bf16[8,48,1024]{2,1,0:T(8,128)(2,1)S(1)} async-done(((bf16[8,48,1024]{2,1,0:T(8,128)(2,1)}), bf16[8,48,1024]{2,1,0:T(8,128)(2,1)S(1)}, u32[]{:S(2)}, u32[]{:S(2)}) %all-to-all-start.1) | async-done | bytes 786464 | tf_op jit(solution)/shard_map/all_to_all | solution.py:38
  37.2 3.1 %scatter_custom_fusion.1 = bf16[384,1024]{1,0:T(8,128)(2,1)} fusion(s32[384]{0:T(512)S(1)} %fusion.19, bf16[384,1024]{1,0:T(8,128)(2,1)S(1)} %bitcast.19, bf16[]{:T(256)} %constant.61.clone.1), kind=kCustom, calls=%fused_computation.20 | custom fusion | bytes 786434 | tf_op jit(solution)/shard_map/scatter | solution.py:56
  40.3 0.7 fusion.20
  41.0 0.6 convert_convert_fusion
  41.6 12.2 %all-gather = bf16[4,1,384]{2,1,0:T(2,128)(2,1)S(1)} all-gather(bf16[1,1,384]{2,1,0:T(2,128)(2,1)S(1)} %reshape.144), channel_id=1, replica_groups=mesh['wide'=8,'grp'=4] {'grp'}, dimensions={0}, use_global_device_ids=true | all-gather | bytes 3840 | tf_op jit(solution)/shard_map/all_gather | solution.py:64
  53.8 49.5 %all-gather.3.cloned.1.call-done = bf16[1536,1024]{1,0:T(8,128)(2,1)} async-done(((bf16[384,1024]{1,0:T(8,128)(2,1)}), bf16[1536,1024]{1,0:T(8,128)(2,1)}) %all-gather.3.cloned.1.call-update) | async-done | bytes 3145744 | tf_op jit(solution)/shard_map/all_gather | solution.py:63
  103.3 16.6 %while.13 = (s32[]{:T(128)}, f32[384]{0:T(512)S(1)}, s32[]{:T(128)}, s32[4]{0:T(128)S(1)}, bf16[1536,1024]{1,0:T(8,128)(2,1)}, /*index=5*/bf16[384,1024]{1,0:T(8...) while((s32[]{:T(128)}, f32[384]{0:T(512)S(1)}, ...), condition=%wide.region_14.15_spmd, body=%wide.region_10.14_spmd.sunk | while | flops 302582016 | bytes 1584705 | solution.py:84
  104.0 0.6 dynamic_slice.15
  105.2 2.1 %conditional.2 = (f32[384]{0:T(512)S(1)}) conditional(s32[]{:T(128)} %convert_element_type.49, f32[384]{0:T(512)S(1)} %get-tuple-element.157, (s32[]{:T(128)}, bf16[1536,1024]{1,0:T(8,128)(2,1)}, bf16[384,1024]{1,0:T(8,128)(2,1)}, bf16[1536]{0:T(1024)(128)(2,1)S(1)}, f32[384]{0:T(512)S(1)}) %tuple.31), branch_computations={%region_11.11_spmd, %region_12.13_spmd} | conditional | flops 302582016 | bytes 1584436 | solution.py:82
  105.3 2.0 %fusion.3 = f32[384]{0:T(512)S(1)} fusion(bf16[384,1024]{1,0:T(8,128)(2,1)} %get-tuple-element.68, bf16[1536,1024]{1,0:T(8,128)(2,1)} %get-tuple-element.66, s32[]{:T(128)S(6)} %min.5, f32[384]{0:T(512)S(1)} %convert_select_fusion), kind=kOutput, calls=%fused_computation.6 | convolution fusion | flops 302579328 | bytes 1575940 | tf_op jit(solution)/shard_map/while/body/cond/branch_1_fun/dot_general | solution.py:14
  108.0 0.6 dynamic_slice.15
  109.2 2.1 %conditional.2 = (f32[384]{0:T(512)S(1)}) conditional(s32[]{:T(128)} %convert_element_type.49, f32[384]{0:T(512)S(1)} %get-tuple-element.157, (s32[]{:T(128)}, bf16[1536,1024]{1,0:T(8,128)(2,1)}, bf16[384,1024]{1,0:T(8,128)(2,1)}, bf16[1536]{0:T(1024)(128)(2,1)S(1)}, f32[384]{0:T(512)S(1)}) %tuple.31), branch_computations={%region_11.11_spmd, %region_12.13_spmd} | conditional | flops 302582016 | bytes 1584436 | solution.py:82
  109.3 2.0 %fusion.3 = f32[384]{0:T(512)S(1)} fusion(bf16[384,1024]{1,0:T(8,128)(2,1)} %get-tuple-element.68, bf16[1536,1024]{1,0:T(8,128)(2,1)} %get-tuple-element.66, s32[]{:T(128)S(6)} %min.5, f32[384]{0:T(512)S(1)} %convert_select_fusion), kind=kOutput, calls=%fused_computation.6 | convolution fusion | flops 302579328 | bytes 1575940 | tf_op jit(solution)/shard_map/while/body/cond/branch_1_fun/dot_general | solution.py:14
  112.0 0.6 dynamic_slice.15
  113.2 2.1 %conditional.2 = (f32[384]{0:T(512)S(1)}) conditional(s32[]{:T(128)} %convert_element_type.49, f32[384]{0:T(512)S(1)} %get-tuple-element.157, (s32[]{:T(128)}, bf16[1536,1024]{1,0:T(8,128)(2,1)}, bf16[384,1024]{1,0:T(8,128)(2,1)}, bf16[1536]{0:T(1024)(128)(2,1)S(1)}, f32[384]{0:T(512)S(1)}) %tuple.31), branch_computations={%region_11.11_spmd, %region_12.13_spmd} | conditional | flops 302582016 | bytes 1584436 | solution.py:82
  113.3 2.0 %fusion.3 = f32[384]{0:T(512)S(1)} fusion(bf16[384,1024]{1,0:T(8,128)(2,1)} %get-tuple-element.68, bf16[1536,1024]{1,0:T(8,128)(2,1)} %get-tuple-element.66, s32[]{:T(128)S(6)} %min.5, f32[384]{0:T(512)S(1)} %convert_select_fusion), kind=kOutput, calls=%fused_computation.6 | convolution fusion | flops 302579328 | bytes 1575940 | tf_op jit(solution)/shard_map/while/body/cond/branch_1_fun/dot_general | solution.py:14
  116.0 0.6 dynamic_slice.15
  117.2 2.1 %conditional.2 = (f32[384]{0:T(512)S(1)}) conditional(s32[]{:T(128)} %convert_element_type.49, f32[384]{0:T(512)S(1)} %get-tuple-element.157, (s32[]{:T(128)}, bf16[1536,1024]{1,0:T(8,128)(2,1)}, bf16[384,1024]{1,0:T(8,128)(2,1)}, bf16[1536]{0:T(1024)(128)(2,1)S(1)}, f32[384]{0:T(512)S(1)}) %tuple.31), branch_computations={%region_11.11_spmd, %region_12.13_spmd} | conditional | flops 302582016 | bytes 1584436 | solution.py:82
  117.3 2.0 %fusion.3 = f32[384]{0:T(512)S(1)} fusion(bf16[384,1024]{1,0:T(8,128)(2,1)} %get-tuple-element.68, bf16[1536,1024]{1,0:T(8,128)(2,1)} %get-tuple-element.66, s32[]{:T(128)S(6)} %min.5, f32[384]{0:T(512)S(1)} %convert_select_fusion), kind=kOutput, calls=%fused_computation.6 | convolution fusion | flops 302579328 | bytes 1575940 | tf_op jit(solution)/shard_map/while/body/cond/branch_1_fun/dot_general | solution.py:14
  120.0 0.6 fusion.18
  120.6 0.6 reshape.125
  (26 shorter events, 1.0 us)
Async XLA Ops:
  9.9 10.5 %all-to-all-start = ((s32[8,1,1]{2,1,0:T(1,128)}), s32[8,1,1]{2,1,0:T(1,128)S(1)}, u32[]{:S(2)}, u32[]{:S(2)}) async-start(s32[8,1,1]{2,1,0:T(1,128)} %copy.5), calls=%async_computation | async-start | bytes 8192 | tf_op jit(solution)/shard_map/all_to_all | solution.py:45
  20.4 16.8 %all-to-all-start.1 = ((bf16[8,48,1024]{2,1,0:T(8,128)(2,1)}), bf16[8,48,1024]{2,1,0:T(8,128)(2,1)S(1)}, u32[]{:S(2)}, u32[]{:S(2)}) async-start(bf16[8,48,1024]{2,1,0:T(8,128)(2,1)} %bitcast.6), calls=%async_computation.1 | async-start | bytes 1572864 | tf_op jit(solution)/shard_map/all_to_all | solution.py:38
  24.6 15.7 %copy-start = (s32[4]{0:T(128)S(1)}, s32[4]{0:T(128)}, u32[]{:S(2)}) copy-start(s32[4]{0:T(128)} %param.9) | copy-start | bytes 52
  24.6 78.8 %all-gather.3.cloned.1.call-start = ((), (), s32[]{:S(2)}) async-start(), calls=%async_computation.2 | async-start | bytes 3932160 | tf_op jit(solution)/shard_map/all_gather | solution.py:63
Sparse Core Ops, SparseCore 0:
  40.4 62.8 all-gather.2
where the time goes:
time: 128 us
  waiting for transfers between devices  60.9 us (48%)
  between operations  13.5 us (11%)
  blocking collectives  12.2 us (10%)
  other arithmetic  11.2 us (9%)
  starting transfers between devices  9.41 us (7%)
  matrix products  8.01 us (6%)
  local copies, waits for them, and re-layouts  7.14 us (6%)
  loops' own time  5.73 us (4%)
    all_gather x1, waiting for transfers between devices, per_device(): panel_rows = lax.all_gather(own_block, 'grp', axis=0, tiled=True)  49.5 us
    all_gather x1, blocking collectives, per_device(): panel_flags = lax.all_gather(flags_wire, 'grp', axis=0, tiled=True)  12.2 us
    all_to_all x1, waiting for transfers between devices, per_device(): lax.all_to_all(outgoing.reshape(wide_count, capacity, feature_width), 'wi...  11.4 us
    dot_general x4, matrix products, pair_sums(): lax.dot_general(left_rows, right_rows, (((1,), (1,)), ((), ())), preferre...  8.01 us
    another operation x1, loops' own time, per_device(): lax.fori_loop(0, live_count, add_pair, jnp.zeros((BLK,), jnp.float32))  5.64 us
    all_to_all x1, starting transfers between devices, per_device(): lax.all_to_all(counts.reshape(wide_count, 1), 'wide', split_axis=0, conca...  5.17 us
    all_to_all x1, starting transfers between devices, per_device(): lax.all_to_all(outgoing.reshape(wide_count, capacity, feature_width), 'wi...  4.2 us
    scatter x1, other arithmetic, per_device(): outgoing = jnp.zeros((wide_count * capacity, feature_width), jnp.bfloat16...  3.3 us
  transfers between devices with their start and end apart: 3, of which 2 were waited for; matrix products, arithmetic and copies ran while one was open for 6% of the time, Pallas kernels for 0%

commit v1 on v0

--- a/solution.py
+++ b/solution.py
@@ -1,7 +1,11 @@
 import jax
 import jax.numpy as jnp
 from jax import lax
+from jax.experimental import pallas as pl
+from jax.experimental.pallas import tpu as pltpu
 from jax.sharding import PartitionSpec as P
+import functools
+import math
 
 BLK = 384
 
@@ -85,8 +89,263 @@
     return (density * valid_rows).reshape(1, BLK)
 
 
-def solution(mesh):
+def general(mesh):
     placed = (P(("wide", "grp"), None), P(("wide", "grp")), P(("wide", "grp")))
     return jax.shard_map(
         per_device, mesh=mesh, in_specs=placed, out_specs=P(("wide", "grp"), None), check_vma=False
     )
+
+
+MESH = pl.DeviceIdType.MESH
+SCALE = SHARPNESS * math.log2(math.e)
+NEVER = -1e30
+MARK = 4.0
+HALVES = 2
+
+
+def rows_times_rows(left, right, precision=None):
+    return lax.dot_general(
+        left, right, (((1,), (1,)), ((), ())), precision=precision,
+        preferred_element_type=jnp.float32,
+    )
+
+
+def gather_kernel(
+    n_wide, n_grp, cap, embeds_ref, bucket_ref, pairs_ref, out_ref,
+    rows, outgoing, panel, part, sums, result,
+    load_sem, send_sem, recv_sem, give_sem, take_sem,
+):
+    me_wide, me_grp = lax.axis_index("wide"), lax.axis_index("grp")
+    parity = lax.rem(me_wide, 2)
+    my_home = n_grp // 2 - parity
+    is_home = me_grp == my_home
+    row_dev, width = rows.shape
+    block = n_wide * cap
+    devices = n_wide * n_grp
+
+    def home_of(bucket_index):
+        return n_grp // 2 - lax.rem(bucket_index, 2)
+
+    def order_of(grp, odd):
+        along = grp + odd * (n_grp - 1 - 2 * grp)
+        return jnp.where(along >= n_grp // 2, along - n_grp // 2, n_grp - 1 - along)
+
+    def grp_of(order, odd):
+        along = order + n_grp // 2 if order < n_grp // 2 else n_grp - 1 - order
+        return along + odd * (n_grp - 1 - 2 * along)
+
+    load = pltpu.make_async_copy(embeds_ref, rows, load_sem)
+    load.start()
+    barrier = pltpu.get_barrier_semaphore()
+
+    @pl.when(is_home)
+    def _():
+        def greet(step, carry):
+            other = lax.rem(me_wide * n_grp + me_grp + step, devices)
+            pl.semaphore_signal(
+                barrier, inc=1, device_id=(other // n_grp, lax.rem(other, n_grp)),
+                device_id_type=MESH,
+            )
+            return carry
+
+        lax.fori_loop(1, devices, greet, 0)
+
+    @pl.when(jnp.logical_not(is_home))
+    def _():
+        pl.semaphore_signal(
+            barrier, inc=1, device_id=(me_wide, my_home), device_id_type=MESH
+        )
+
+    bucket = bucket_ref[...]
+    of_bucket = lax.broadcasted_iota(jnp.int32, (n_wide, row_dev), 0) == bucket
+    onehot = of_bucket.astype(jnp.float32)
+    earlier = (
+        lax.broadcasted_iota(jnp.int32, (row_dev, row_dev), 0)
+        < lax.broadcasted_iota(jnp.int32, (row_dev, row_dev), 1)
+    ).astype(jnp.float32).astype(jnp.bfloat16)
+    before = jnp.dot(onehot.astype(jnp.bfloat16), earlier, preferred_element_type=jnp.float32)
+    rank = jnp.sum(before * onehot, axis=0, keepdims=True).astype(jnp.int32)
+    counts = jnp.sum(onehot, axis=1, keepdims=True).astype(jnp.int32)
+    slots = bucket * cap + rank
+    chosen = (
+        lax.broadcasted_iota(jnp.int32, (block, row_dev), 0) == slots
+    ).astype(jnp.float32).astype(jnp.bfloat16)
+
+    load.wait()
+    floats = rows[...].astype(jnp.float32)
+    unit = (
+        floats * lax.rsqrt(jnp.sum(floats * floats, axis=1, keepdims=True) + EPSILON)
+    ).astype(jnp.bfloat16)
+    placed = jnp.dot(chosen, unit, preferred_element_type=jnp.float32)
+    first_lane = lax.broadcasted_iota(jnp.int32, (cap, 128), 1) == 0
+    within = lax.broadcasted_iota(jnp.int32, (cap, 128), 0)
+    for o in range(n_wide):
+        piece = placed[o * cap : (o + 1) * cap]
+        padding = first_lane & (within >= counts[o : o + 1, :])
+        outgoing[o, :, :128] = jnp.where(padding, MARK, piece[:, :128]).astype(jnp.bfloat16)
+        outgoing[o, :, 128:] = piece[:, 128:].astype(jnp.bfloat16)
+
+    @pl.when(is_home)
+    def _():
+        pl.semaphore_wait(barrier, n_wide - 1 + n_grp - 1)
+
+    @pl.when(jnp.logical_not(is_home))
+    def _():
+        pl.semaphore_wait(barrier, n_wide)
+
+    def piece_copy(o):
+        place = order_of(me_grp, lax.rem(o, 2)) * n_wide + me_wide
+        return pltpu.make_async_remote_copy(
+            src_ref=outgoing.at[o], dst_ref=panel.at[place],
+            send_sem=send_sem.at[o], recv_sem=recv_sem.at[place],
+            device_id=(o, home_of(o)), device_id_type=MESH,
+        )
+
+    for step in range(1, n_wide):
+        piece_copy(lax.rem(me_wide + step, n_wide)).start()
+
+    @pl.when(jnp.logical_not(is_home))
+    def _():
+        piece_copy(me_wide).start()
+
+    @pl.when(is_home)
+    def _():
+        place = order_of(me_grp, parity) * n_wide + me_wide
+        own = pltpu.make_async_copy(outgoing.at[me_wide], panel.at[place], recv_sem.at[place])
+        own.start()
+        unit_pieces = n_wide // HALVES
+        unit_rows = block // HALVES
+        lane_bias = []
+        pick = (
+            (lax.broadcasted_iota(jnp.int32, (8, 128), 1) == 0)
+            .astype(jnp.float32).astype(jnp.bfloat16)
+        )
+        ones = jnp.ones((8, 128), jnp.float32)
+        for k in range(n_grp):
+            row_bias = []
+            for h in range(HALVES):
+                first = k * n_wide + h * unit_pieces
+                for p in range(first, first + unit_pieces):
+                    pltpu.make_async_copy(panel.at[p], panel.at[p], recv_sem.at[p]).wait()
+                left = panel[first : first + unit_pieces].reshape(unit_rows, width)
+                bias = jnp.where(left[:, 0:1].astype(jnp.float32) < 2.0, -SCALE, NEVER)
+                row_bias.append(bias)
+                for b in range(k):
+                    right = panel[b * n_wide : (b + 1) * n_wide].reshape(block, width)
+                    e = jnp.exp2(rows_times_rows(left, right) * SCALE + bias + lane_bias[b])
+                    down = jnp.sum(e, axis=0, keepdims=True)
+                    if h == 0:
+                        sums[b, k : k + 1, :] = down
+                    else:
+                        sums[b, k : k + 1, :] += down
+                    folded = e[:, :128]
+                    for lane in range(128, block, 128):
+                        folded = folded + e[:, lane : lane + 128]
+                    part[b, h * unit_rows : (h + 1) * unit_rows, :] = folded
+            whole = panel[k * n_wide : (k + 1) * n_wide].reshape(block, width)
+            valid = rows_times_rows(pick, whole[:, :128])[0:1] < 2.0
+            lane_bias.append(jnp.where(valid, 0.0, NEVER))
+            own_sum = jnp.zeros((1, block), jnp.float32)
+            for h in range(HALVES):
+                left = panel[
+                    k * n_wide + h * unit_pieces : k * n_wide + (h + 1) * unit_pieces
+                ].reshape(unit_rows, width)
+                e = jnp.exp2(rows_times_rows(left, whole) * SCALE + row_bias[h] + lane_bias[k])
+                own_sum = own_sum + jnp.sum(e, axis=0, keepdims=True)
+            sums[k, k : k + 1, :] = own_sum
+            sums[k, n_grp : n_grp + 1, :] = valid.astype(jnp.float32)
+            for b in range(k):
+                across = rows_times_rows(ones, part[b], lax.Precision.HIGHEST)
+                sums[k, b : b + 1, :] = across[0:1]
+
+        keep = pltpu.make_async_copy(sums.at[0], result, take_sem)
+        keep.start()
+        gives = []
+        for k in range(1, n_grp):
+            give = pltpu.make_async_remote_copy(
+                src_ref=sums.at[k], dst_ref=result,
+                send_sem=give_sem.at[k], recv_sem=take_sem,
+                device_id=(me_wide, grp_of(k, parity)), device_id_type=MESH,
+            )
+            give.start()
+            gives.append(give)
+        for give in gives:
+            give.wait_send()
+
+    sooner = (
+        lax.broadcasted_iota(jnp.int32, (block, block), 0)
+        < lax.broadcasted_iota(jnp.int32, (block, block), 1)
+    ).astype(jnp.float32).astype(jnp.bfloat16)
+    position = lax.broadcasted_iota(jnp.int32, (block, block), 0)
+    weights = []
+    for k in range(n_grp):
+        named = grp_of(k, parity)
+        weight = jnp.float32(0.0)
+        for p in range(pairs_ref.shape[0]):
+            weight = weight + jnp.where(pairs_ref[p] == named, 1.0, 0.0)
+        weights.append(weight)
+    pltpu.make_async_copy(result, result, take_sem).wait()
+    got = result[...]
+    flags = got[n_grp : n_grp + 1]
+    ahead = jnp.dot(
+        jnp.broadcast_to(flags, (8, block)).astype(jnp.bfloat16), sooner,
+        preferred_element_type=jnp.float32,
+    )[0:1]
+    slot_place = jnp.where(flags > 0.5, ahead, -1.0).astype(jnp.int32)
+    squeeze = (position == slot_place).astype(jnp.float32)
+    total = jnp.zeros((1, block), jnp.float32)
+    for k in range(n_grp):
+        total = total + got[k : k + 1] * weights[k]
+    out_ref[...] = rows_times_rows(
+        jnp.broadcast_to(total, (8, block)), squeeze, lax.Precision.HIGHEST
+    )[0:1]
+
+    for o in range(n_wide):
+        @pl.when(jnp.logical_not(is_home & (me_wide == o)))
+        def _():
+            piece_copy(o).wait_send()
+
+
+def gathered(embeds, bucket, pairs):
+    n_wide, n_grp = lax.axis_size("wide"), lax.axis_size("grp")
+    row_dev, width = embeds.shape
+    cap = BLK // n_wide
+    vmem = pl.BlockSpec(memory_space=pltpu.VMEM)
+    return pl.pallas_call(
+        functools.partial(gather_kernel, n_wide, n_grp, cap),
+        out_shape=jax.ShapeDtypeStruct((1, BLK), jnp.float32),
+        in_specs=[
+            pl.BlockSpec(memory_space=pl.ANY), vmem, pl.BlockSpec(memory_space=pltpu.SMEM)
+        ],
+        out_specs=vmem,
+        scratch_shapes=[
+            pltpu.VMEM((row_dev, width), embeds.dtype),
+            pltpu.VMEM((n_wide, cap, width), jnp.bfloat16),
+            pltpu.VMEM((n_wide * n_grp, cap, width), jnp.bfloat16),
+            pltpu.VMEM((n_grp, BLK, 128), jnp.float32),
+            pltpu.VMEM((n_grp, 8, BLK), jnp.float32),
+            pltpu.VMEM((8, BLK), jnp.float32),
+            pltpu.SemaphoreType.DMA,
+            pltpu.SemaphoreType.DMA((n_wide,)),
+            pltpu.SemaphoreType.DMA((n_wide * n_grp,)),
+            pltpu.SemaphoreType.DMA((n_grp,)),
+            pltpu.SemaphoreType.DMA,
+        ],
+        compiler_params=pltpu.CompilerParams(
+            collective_id=0, has_side_effects=True, vmem_limit_bytes=40 * 1024 * 1024
+        ),
+        cost_estimate=pl.CostEstimate(
+            flops=20 * BLK * BLK * width, bytes_accessed=2 * row_dev * width,
+            transcendentals=10 * BLK * BLK,
+        ),
+    )(embeds, bucket.reshape(1, row_dev), pairs)
+
+
+def solution(mesh):
+    n_wide, n_grp = mesh.shape["wide"], mesh.shape["grp"]
+    if n_grp != 4 or (BLK // n_wide) % 16:
+        return general(mesh)
+    placed = (P(("wide", "grp"), None), P(("wide", "grp")), P(("wide", "grp")))
+    return jax.shard_map(
+        gathered, mesh=mesh, in_specs=placed, out_specs=P(("wide", "grp"), None), check_vma=False
+    )

time: 128 us -> 41.9 us (0.33)
  waiting for transfers between devices: 60.9 us -> 0 us
  Pallas kernels: 0 us -> 39.4 us
  between operations: 13.5 us -> 0.01 us
  blocking collectives: 12.2 us -> 0 us
  other arithmetic: 11.2 us -> 0 us
  starting transfers between devices: 9.41 us -> 0 us
  matrix products: 8.01 us -> 0 us
  loops' own time: 5.73 us -> 0 us
  local copies, waits for them, and re-layouts: 7.14 us -> 2.33 us
    all_gather x1 -> x0, waiting for transfers between devices: 49.5 us -> none  [per_device(): panel_rows = lax.all_gather(own_block, 'grp', axis=0, tiled=True)]
    pallas_call x0 -> x1, Pallas kernels: none -> 39.4 us  [gathered(): pl.pallas_call(functools.partial(gather_kernel, n_wide, n_grp, cap), out_...]
    all_gather x1 -> x0, blocking collectives: 12.2 us -> none  [per_device(): panel_flags = lax.all_gather(flags_wire, 'grp', axis=0, tiled=True)]
    all_to_all x2 -> x0, waiting for transfers between devices: 11.4 us -> none  [the longest x1 11.4 us: per_device(): lax.all_to_all(outgoing.reshape(wide_count, capacity, feature_width), 'wi...]
    all_to_all x2 -> x0, starting transfers between devices: 9.37 us -> none  [the longest x1 5.17 us: per_device(): lax.all_to_all(counts.reshape(wide_count, 1), 'wide', split_axis=0, conca...]
    dot_general x4 -> x0, matrix products: 8.01 us -> none  [pair_sums(): lax.dot_general(left_rows, right_rows, (((1,), (1,)), ((), ())), preferre...]
    another operation x5 -> x0, loops' own time: 5.73 us -> none  [the longest x1 5.64 us: per_device(): lax.fori_loop(0, live_count, add_pair, jnp.zeros((BLK,), jnp.float32))]
    reduce_sum x4 -> x0, other arithmetic: 3.56 us -> none  [the longest x1 1.27 us: per_device(): jnp.sum(floats * floats, axis=1, keepdims=True) + EPSILON]
  transfers between devices with their start and end apart: 3 -> 0, of which waited for: 2 -> 0; matrix products, arithmetic and copies ran while one was open for 6% -> 0% of each run, Pallas kernels for 0% -> 0%
where the time goes in v1:
time: 41.9 us; the launch traced here: 41.7 us
  Pallas kernels  39.4 us (94%)
  local copies, waits for them, and re-layouts  2.33 us (6%)
    pallas_call x1, Pallas kernels, gathered(): pl.pallas_call(functools.partial(gather_kernel, n_wide, n_grp, cap), out_...  39.4 us
    unnamed x5, local copies, waits for them, and re-layouts  1.63 us

profile of v1, /device:TPU:0, one launch (start us, length us, event | category | flops | bytes accessed | tf_op | source)
XLA Modules:
  0.0 41.7 jit_solution(12345198918221175788)
XLA Ops:
  0.0 0.0 copy-start.1
  0.0 0.7 %reshape.3.bucket_ref = s32[1,288]{1,0:T(1,128)S(1)} reshape(s32[288]{0:T(512)} %param.4) | data formatting | bytes 2304 | tf_op jit(solution)/shard_map/reshape | solution.py:341
  0.7 0.0 copy-done.1
  0.7 0.0 copy-start
  0.7 1.1 %copy-done = bf16[288,1024]{1,0:T(8,128)(2,1)S(1)} copy-done((bf16[288,1024]{1,0:T(8,128)(2,1)S(1)}, bf16[288,1024]{1,0:T(8,128)(2,1)}, u32[]{:S(2)}) %copy-start) | copy-done | bytes 589848
  1.8 39.4 %shard_map.37 = f32[1,384]{1,0:T(1,128)S(1)} custom-call(bf16[288,1024]{1,0:T(8,128)(2,1)S(1)} %copy-done, s32[1,288]{1,0:T(1,128)S(1)} %reshape.3.bucket_ref, s32[4]{0:T(128)S(1)} %copy-done.1), custom_call_target="tpu_custom_call" | custom-call | flops 3019898880 | bytes 589824 | tf_op jit(solution)/shard_map/pallas_call | solution.py:314
  41.2 0.6 %copy.5 = f32[1,384]{1,0:T(1,128)} copy(f32[1,384]{1,0:T(1,128)S(1)} %shard_map.37) | data formatting | bytes 3072
Async XLA Ops:
  0.0 0.7 %copy-start.1 = (s32[4]{0:T(128)S(1)}, s32[4]{0:T(128)}, u32[]{:S(2)}) copy-start(s32[4]{0:T(128)} %pairs_ref.1) | copy-start | bytes 52
  0.7 1.1 %copy-start = (bf16[288,1024]{1,0:T(8,128)(2,1)S(1)}, bf16[288,1024]{1,0:T(8,128)(2,1)}, u32[]{:S(2)}) copy-start(bf16[288,1024]{1,0:T(8,128)(2,1)} %embeds_ref.1) | copy-start | bytes 1769476

commit v2 on v1

--- a/solution.py
+++ b/solution.py
@@ -100,7 +100,6 @@
 SCALE = SHARPNESS * math.log2(math.e)
 NEVER = -1e30
 MARK = 4.0
-HALVES = 2
 
 
 def rows_times_rows(left, right, precision=None):
@@ -110,9 +109,17 @@
     )
 
 
+def thirds(values, axis):
+    high = values.astype(jnp.bfloat16)
+    rest = values - high.astype(jnp.float32)
+    middle = rest.astype(jnp.bfloat16)
+    low = (rest - middle.astype(jnp.float32)).astype(jnp.bfloat16)
+    return jnp.concatenate([high, middle, low], axis=axis)
+
+
 def gather_kernel(
     n_wide, n_grp, cap, embeds_ref, bucket_ref, pairs_ref, out_ref,
-    rows, outgoing, panel, part, sums, result,
+    rows, bucket_row, entries, outgoing, panel, sums, result,
     load_sem, send_sem, recv_sem, give_sem, take_sem,
 ):
     me_wide, me_grp = lax.axis_index("wide"), lax.axis_index("grp")
@@ -122,9 +129,7 @@
     row_dev, width = rows.shape
     block = n_wide * cap
     devices = n_wide * n_grp
-
-    def home_of(bucket_index):
-        return n_grp // 2 - lax.rem(bucket_index, 2)
+    half = n_wide // 2
 
     def order_of(grp, odd):
         along = grp + odd * (n_grp - 1 - 2 * grp)
@@ -134,8 +139,12 @@
         along = order + n_grp // 2 if order < n_grp // 2 else n_grp - 1 - order
         return along + odd * (n_grp - 1 - 2 * along)
 
-    load = pltpu.make_async_copy(embeds_ref, rows, load_sem)
+    load = pltpu.make_async_copy(embeds_ref, rows, load_sem.at[0])
     load.start()
+    load_bucket = pltpu.make_async_copy(bucket_ref, bucket_row, load_sem.at[1])
+    load_bucket.start()
+    load_pairs = pltpu.make_async_copy(pairs_ref, entries, load_sem.at[2])
+    load_pairs.start()
     barrier = pltpu.get_barrier_semaphore()
 
     @pl.when(is_home)
@@ -156,7 +165,8 @@
             barrier, inc=1, device_id=(me_wide, my_home), device_id_type=MESH
         )
 
-    bucket = bucket_ref[...]
+    load_bucket.wait()
+    bucket = bucket_row[...].reshape(1, row_dev)
     of_bucket = lax.broadcasted_iota(jnp.int32, (n_wide, row_dev), 0) == bucket
     onehot = of_bucket.astype(jnp.float32)
     earlier = (
@@ -166,24 +176,45 @@
     before = jnp.dot(onehot.astype(jnp.bfloat16), earlier, preferred_element_type=jnp.float32)
     rank = jnp.sum(before * onehot, axis=0, keepdims=True).astype(jnp.int32)
     counts = jnp.sum(onehot, axis=1, keepdims=True).astype(jnp.int32)
-    slots = bucket * cap + rank
-    chosen = (
-        lax.broadcasted_iota(jnp.int32, (block, row_dev), 0) == slots
-    ).astype(jnp.float32).astype(jnp.bfloat16)
+    slots = (bucket >> 1) * cap + rank
 
     load.wait()
     floats = rows[...].astype(jnp.float32)
     unit = (
         floats * lax.rsqrt(jnp.sum(floats * floats, axis=1, keepdims=True) + EPSILON)
     ).astype(jnp.bfloat16)
-    placed = jnp.dot(chosen, unit, preferred_element_type=jnp.float32)
     first_lane = lax.broadcasted_iota(jnp.int32, (cap, 128), 1) == 0
     within = lax.broadcasted_iota(jnp.int32, (cap, 128), 0)
-    for o in range(n_wide):
-        piece = placed[o * cap : (o + 1) * cap]
-        padding = first_lane & (within >= counts[o : o + 1, :])
-        outgoing[o, :, :128] = jnp.where(padding, MARK, piece[:, :128]).astype(jnp.bfloat16)
-        outgoing[o, :, 128:] = piece[:, 128:].astype(jnp.bfloat16)
+
+    odd_of = [1 - lax.rem(me_grp, 2), lax.rem(me_grp, 2)]
+
+    def fill(turn):
+        odd = odd_of[turn]
+        mine = jnp.where((bucket & 1) == odd, slots, -1)
+        chosen = (
+            lax.broadcasted_iota(jnp.int32, (half * cap, row_dev), 0) == mine
+        ).astype(jnp.float32).astype(jnp.bfloat16)
+        placed = jnp.dot(chosen, unit, preferred_element_type=jnp.float32)
+        for m in range(half):
+            piece = placed[m * cap : (m + 1) * cap]
+            held = jnp.where(odd == 0, counts[2 * m : 2 * m + 1], counts[2 * m + 1 : 2 * m + 2])
+            padding = first_lane & (within >= held)
+            at = turn * half + m
+            outgoing[at, :, :128] = jnp.where(padding, MARK, piece[:, :128]).astype(jnp.bfloat16)
+            outgoing[at, :, 128:] = piece[:, 128:].astype(jnp.bfloat16)
+
+    def piece_copy(turn, step):
+        odd = odd_of[turn]
+        m = lax.rem(me_wide // 2 + step, half)
+        place = order_of(me_grp, odd) * n_wide + me_wide
+        return pltpu.make_async_remote_copy(
+            src_ref=outgoing.at[turn * half + m],
+            dst_ref=panel.at[pl.ds(pl.multiple_of(place * cap, cap), cap)],
+            send_sem=send_sem.at[turn * half + m], recv_sem=recv_sem.at[place],
+            device_id=(2 * m + odd, n_grp // 2 - odd), device_id_type=MESH,
+        )
+
+    fill(0)
 
     @pl.when(is_home)
     def _():
@@ -193,70 +224,94 @@
     def _():
         pl.semaphore_wait(barrier, n_wide)
 
-    def piece_copy(o):
-        place = order_of(me_grp, lax.rem(o, 2)) * n_wide + me_wide
-        return pltpu.make_async_remote_copy(
-            src_ref=outgoing.at[o], dst_ref=panel.at[place],
-            send_sem=send_sem.at[o], recv_sem=recv_sem.at[place],
-            device_id=(o, home_of(o)), device_id_type=MESH,
-        )
-
-    for step in range(1, n_wide):
-        piece_copy(lax.rem(me_wide + step, n_wide)).start()
-
-    @pl.when(jnp.logical_not(is_home))
-    def _():
-        piece_copy(me_wide).start()
+    for step in range(half):
+        piece_copy(0, step).start()
+    fill(1)
+
+    is_end = (me_grp == 0) | (me_grp == n_grp - 1)
+
+    @pl.when(is_end)
+    def _():
+        for step in range(half):
+            piece_copy(0, step).wait_send()
+            piece_copy(1, step).start()
+
+    @pl.when(jnp.logical_not(is_end))
+    def _():
+        for step in range(1, half):
+            piece_copy(1, step).start()
+
+        @pl.when(jnp.logical_not(is_home))
+        def _():
+            piece_copy(1, 0).start()
+
+    def arrive(place):
+        slot = panel.at[place * cap : (place + 1) * cap]
+        pltpu.make_async_copy(slot, slot, recv_sem.at[place]).wait()
 
     @pl.when(is_home)
     def _():
         place = order_of(me_grp, parity) * n_wide + me_wide
-        own = pltpu.make_async_copy(outgoing.at[me_wide], panel.at[place], recv_sem.at[place])
-        own.start()
-        unit_pieces = n_wide // HALVES
-        unit_rows = block // HALVES
-        lane_bias = []
+        pltpu.make_async_copy(
+            outgoing.at[half + me_wide // 2],
+            panel.at[pl.ds(pl.multiple_of(place * cap, cap), cap)],
+            recv_sem.at[place],
+        ).start()
         pick = (
             (lax.broadcasted_iota(jnp.int32, (8, 128), 1) == 0)
             .astype(jnp.float32).astype(jnp.bfloat16)
         )
-        ones = jnp.ones((8, 128), jnp.float32)
+        ones = jnp.ones((8, 3 * 128), jnp.bfloat16)
+
+        def lane_flags(first, count):
+            return rows_times_rows(pick, panel[first : first + count, :128])[0:1] < 2.0
+
+        def fold(e, lanes):
+            folded = e[:, :128]
+            for lane in range(128, lanes, 128):
+                folded = folded + e[:, lane : lane + 128]
+            return folded
+
+        def row_sums(folded):
+            return rows_times_rows(ones, thirds(folded, 1))[0:1]
+
+        lane_bias = []
         for k in range(n_grp):
-            row_bias = []
-            for h in range(HALVES):
-                first = k * n_wide + h * unit_pieces
-                for p in range(first, first + unit_pieces):
-                    pltpu.make_async_copy(panel.at[p], panel.at[p], recv_sem.at[p]).wait()
-                left = panel[first : first + unit_pieces].reshape(unit_rows, width)
+            base = k * block
+            step_rows = 128 if k == n_grp - 1 else block
+            own_bias = []
+            arrived = 0
+            for start in range(0, block, step_rows):
+                stop = start + step_rows
+                while arrived * cap < stop:
+                    arrive(k * n_wide + arrived)
+                    arrived += 1
+                left = panel[base + start : base + stop]
                 bias = jnp.where(left[:, 0:1].astype(jnp.float32) < 2.0, -SCALE, NEVER)
-                row_bias.append(bias)
+                valid = lane_flags(base + start, step_rows)
+                sums[k, n_grp : n_grp + 1, start:stop] = valid.astype(jnp.float32)
+                own_bias.append(jnp.where(valid, 0.0, NEVER))
                 for b in range(k):
-                    right = panel[b * n_wide : (b + 1) * n_wide].reshape(block, width)
+                    right = panel[b * block : (b + 1) * block]
                     e = jnp.exp2(rows_times_rows(left, right) * SCALE + bias + lane_bias[b])
                     down = jnp.sum(e, axis=0, keepdims=True)
-                    if h == 0:
+                    if start == 0:
                         sums[b, k : k + 1, :] = down
                     else:
                         sums[b, k : k + 1, :] += down
-                    folded = e[:, :128]
-                    for lane in range(128, block, 128):
-                        folded = folded + e[:, lane : lane + 128]
-                    part[b, h * unit_rows : (h + 1) * unit_rows, :] = folded
-            whole = panel[k * n_wide : (k + 1) * n_wide].reshape(block, width)
-            valid = rows_times_rows(pick, whole[:, :128])[0:1] < 2.0
-            lane_bias.append(jnp.where(valid, 0.0, NEVER))
-            own_sum = jnp.zeros((1, block), jnp.float32)
-            for h in range(HALVES):
-                left = panel[
-                    k * n_wide + h * unit_pieces : k * n_wide + (h + 1) * unit_pieces
-                ].reshape(unit_rows, width)
-                e = jnp.exp2(rows_times_rows(left, whole) * SCALE + row_bias[h] + lane_bias[k])
-                own_sum = own_sum + jnp.sum(e, axis=0, keepdims=True)
-            sums[k, k : k + 1, :] = own_sum
-            sums[k, n_grp : n_grp + 1, :] = valid.astype(jnp.float32)
-            for b in range(k):
-                across = rows_times_rows(ones, part[b], lax.Precision.HIGHEST)
-                sums[k, b : b + 1, :] = across[0:1]
+                    sums[k, b : b + 1, start:stop] = row_sums(fold(e, block))
+                right = panel[base : base + stop]
+                e = jnp.exp2(
+                    rows_times_rows(left, right) * SCALE + bias
+                    + jnp.concatenate(own_bias, axis=1)
+                )
+                down = jnp.sum(e, axis=0, keepdims=True)
+                if start == 0:
+                    sums[k, k : k + 1, start:stop] = down
+                else:
+                    sums[k, k : k + 1, :start] += down[:, :start]
+                    sums[k, k : k + 1, start:stop] = down[:, start:] + row_sums(fold(e, start))
+            lane_bias.append(jnp.concatenate(own_bias, axis=1))
 
         keep = pltpu.make_async_copy(sums.at[0], result, take_sem)
         keep.start()
@@ -277,12 +332,13 @@
         < lax.broadcasted_iota(jnp.int32, (block, block), 1)
     ).astype(jnp.float32).astype(jnp.bfloat16)
     position = lax.broadcasted_iota(jnp.int32, (block, block), 0)
+    load_pairs.wait()
     weights = []
     for k in range(n_grp):
         named = grp_of(k, parity)
         weight = jnp.float32(0.0)
-        for p in range(pairs_ref.shape[0]):
-            weight = weight + jnp.where(pairs_ref[p] == named, 1.0, 0.0)
+        for p in range(entries.shape[0]):
+            weight = weight + jnp.where(entries[p] == named, 1.0, 0.0)
         weights.append(weight)
     pltpu.make_async_copy(result, result, take_sem).wait()
     got = result[...]
@@ -292,53 +348,56 @@
         preferred_element_type=jnp.float32,
     )[0:1]
     slot_place = jnp.where(flags > 0.5, ahead, -1.0).astype(jnp.int32)
-    squeeze = (position == slot_place).astype(jnp.float32)
+    squeeze = (position == slot_place).astype(jnp.float32).astype(jnp.bfloat16)
     total = jnp.zeros((1, block), jnp.float32)
     for k in range(n_grp):
         total = total + got[k : k + 1] * weights[k]
-    out_ref[...] = rows_times_rows(
-        jnp.broadcast_to(total, (8, block)), squeeze, lax.Precision.HIGHEST
-    )[0:1]
-
-    for o in range(n_wide):
-        @pl.when(jnp.logical_not(is_home & (me_wide == o)))
+    squeezed = rows_times_rows(
+        thirds(jnp.broadcast_to(total, (16, block)), 0), squeeze
+    )
+    out_ref[...] = squeezed[0:1] + squeezed[16:17] + squeezed[32:33]
+
+    for step in range(half):
+        @pl.when(jnp.logical_not(is_end))
         def _():
-            piece_copy(o).wait_send()
+            piece_copy(0, step).wait_send()
+
+        @pl.when(jnp.logical_not(is_home & (step == 0)))
+        def _():
+            piece_copy(1, step).wait_send()
 
 
 def gathered(embeds, bucket, pairs):
     n_wide, n_grp = lax.axis_size("wide"), lax.axis_size("grp")
     row_dev, width = embeds.shape
     cap = BLK // n_wide
-    vmem = pl.BlockSpec(memory_space=pltpu.VMEM)
     return pl.pallas_call(
         functools.partial(gather_kernel, n_wide, n_grp, cap),
         out_shape=jax.ShapeDtypeStruct((1, BLK), jnp.float32),
-        in_specs=[
-            pl.BlockSpec(memory_space=pl.ANY), vmem, pl.BlockSpec(memory_space=pltpu.SMEM)
-        ],
-        out_specs=vmem,
+        in_specs=[pl.BlockSpec(memory_space=pl.ANY)] * 3,
+        out_specs=pl.BlockSpec(memory_space=pltpu.VMEM),
         scratch_shapes=[
             pltpu.VMEM((row_dev, width), embeds.dtype),
+            pltpu.VMEM((row_dev,), jnp.int32),
+            pltpu.SMEM(pairs.shape, jnp.int32),
             pltpu.VMEM((n_wide, cap, width), jnp.bfloat16),
-            pltpu.VMEM((n_wide * n_grp, cap, width), jnp.bfloat16),
-            pltpu.VMEM((n_grp, BLK, 128), jnp.float32),
+            pltpu.VMEM((n_grp * BLK, width), jnp.bfloat16),
             pltpu.VMEM((n_grp, 8, BLK), jnp.float32),
             pltpu.VMEM((8, BLK), jnp.float32),
-            pltpu.SemaphoreType.DMA,
+            pltpu.SemaphoreType.DMA((3,)),
             pltpu.SemaphoreType.DMA((n_wide,)),
             pltpu.SemaphoreType.DMA((n_wide * n_grp,)),
             pltpu.SemaphoreType.DMA((n_grp,)),
             pltpu.SemaphoreType.DMA,
         ],
         compiler_params=pltpu.CompilerParams(
-            collective_id=0, has_side_effects=True, vmem_limit_bytes=40 * 1024 * 1024
+            collective_id=0, has_side_effects=True, vmem_limit_bytes=60 * 1024 * 1024
         ),
         cost_estimate=pl.CostEstimate(
             flops=20 * BLK * BLK * width, bytes_accessed=2 * row_dev * width,
             transcendentals=10 * BLK * BLK,
         ),
-    )(embeds, bucket.reshape(1, row_dev), pairs)
+    )(embeds, bucket, pairs)
 
 
 def solution(mesh):

time: 41.9 us -> 39.3 us (0.938)
  Pallas kernels: 39.4 us -> 37.7 us
  local copies, waits for them, and re-layouts: 2.33 us -> 1.24 us
    pallas_call x1, Pallas kernels: 39.4 us -> 37.7 us  [gathered(): pl.pallas_call(functools.partial(gather_kernel, n_wide, n_grp, cap), out_...]
    reshape x1 -> x0, local copies, waits for them, and re-layouts: 0.7 us -> none  [gathered(): bucket.reshape(1, row_dev)]
    unnamed x5 -> x1, local copies, waits for them, and re-layouts: 1.63 us -> 1.24 us
where the time goes in v2:
time: 39.3 us; the launch traced here: 38.9 us
  Pallas kernels  37.7 us (96%)
  local copies, waits for them, and re-layouts  1.24 us (3%)
    pallas_call x1, Pallas kernels, gathered(): pl.pallas_call(functools.partial(gather_kernel, n_wide, n_grp, cap), out_...  37.7 us
    unnamed x1, local copies, waits for them, and re-layouts  1.24 us

profile of v2, /device:TPU:0, one launch (start us, length us, event | category | flops | bytes accessed | tf_op | source)
XLA Modules:
  0.0 38.9 jit_solution(11772181836600337368)
XLA Ops:
  0.0 37.7 %shard_map.37 = f32[1,384]{1,0:T(1,128)} custom-call(bf16[288,1024]{1,0:T(8,128)(2,1)} %embeds_ref.1, s32[288]{0:T(512)} %bucket_ref.1, s32[4]{0:T(128)} %pairs_ref.1), custom_call_target="tpu_custom_call" | custom-call | flops 3019898880 | bytes 589824 | tf_op jit(solution)/shard_map/pallas_call | solution.py:374
  37.7 1.2 %copy.5 = f32[1,384]{1,0:T(1,128)} copy(f32[1,384]{1,0:T(1,128)} %shard_map.37) | data formatting | bytes 3072

commit v3 on v2

--- a/solution.py
+++ b/solution.py
@@ -206,7 +206,7 @@
     def piece_copy(turn, step):
         odd = odd_of[turn]
         m = lax.rem(me_wide // 2 + step, half)
-        place = order_of(me_grp, odd) * n_wide + me_wide
+        place = order_of(me_grp, odd) * n_wide + 2 * step + parity
         return pltpu.make_async_remote_copy(
             src_ref=outgoing.at[turn * half + m],
             dst_ref=panel.at[pl.ds(pl.multiple_of(place * cap, cap), cap)],
@@ -245,13 +245,32 @@
         def _():
             piece_copy(1, 0).start()
 
+    def shard_order(axis):
+        slot = lax.broadcasted_iota(jnp.int32, (block, block), axis)
+        mine = me_wide // 2
+        step = jnp.zeros((block, block), jnp.int32)
+        for t in range(1, half):
+            step = step + (slot >= 2 * t * cap).astype(jnp.int32)
+        wraps = (step > mine).astype(jnp.int32)
+        return slot + cap * (2 * mine - 4 * step + n_wide * wraps)
+
+    sooner = (shard_order(0) < shard_order(1)).astype(jnp.float32).astype(jnp.bfloat16)
+    load_pairs.wait()
+    weights = []
+    for k in range(n_grp):
+        named = grp_of(k, parity)
+        weight = jnp.float32(0.0)
+        for p in range(entries.shape[0]):
+            weight = weight + jnp.where(entries[p] == named, 1.0, 0.0)
+        weights.append(weight)
+
     def arrive(place):
         slot = panel.at[place * cap : (place + 1) * cap]
         pltpu.make_async_copy(slot, slot, recv_sem.at[place]).wait()
 
     @pl.when(is_home)
     def _():
-        place = order_of(me_grp, parity) * n_wide + me_wide
+        place = order_of(me_grp, parity) * n_wide + parity
         pltpu.make_async_copy(
             outgoing.at[half + me_wide // 2],
             panel.at[pl.ds(pl.multiple_of(place * cap, cap), cap)],
@@ -327,19 +346,6 @@
         for give in gives:
             give.wait_send()
 
-    sooner = (
-        lax.broadcasted_iota(jnp.int32, (block, block), 0)
-        < lax.broadcasted_iota(jnp.int32, (block, block), 1)
-    ).astype(jnp.float32).astype(jnp.bfloat16)
-    position = lax.broadcasted_iota(jnp.int32, (block, block), 0)
-    load_pairs.wait()
-    weights = []
-    for k in range(n_grp):
-        named = grp_of(k, parity)
-        weight = jnp.float32(0.0)
-        for p in range(entries.shape[0]):
-            weight = weight + jnp.where(entries[p] == named, 1.0, 0.0)
-        weights.append(weight)
     pltpu.make_async_copy(result, result, take_sem).wait()
     got = result[...]
     flags = got[n_grp : n_grp + 1]
@@ -348,6 +354,7 @@
         preferred_element_type=jnp.float32,
     )[0:1]
     slot_place = jnp.where(flags > 0.5, ahead, -1.0).astype(jnp.int32)
+    position = lax.broadcasted_iota(jnp.int32, (block, block), 0)
     squeeze = (position == slot_place).astype(jnp.float32).astype(jnp.bfloat16)
     total = jnp.zeros((1, block), jnp.float32)
     for k in range(n_grp):

time: 39.3 us -> 37.7 us (0.959)
  Pallas kernels: 37.7 us -> 36.3 us
    pallas_call x1, Pallas kernels: 37.7 us -> 36.3 us  [gathered(): pl.pallas_call(functools.partial(gather_kernel, n_wide, n_grp, cap), out_...]
where the time goes in v3:
time: 37.7 us; the launch traced here: 37.6 us
  Pallas kernels  36.3 us (96%)
  local copies, waits for them, and re-layouts  1.24 us (3%)
    pallas_call x1, Pallas kernels, gathered(): pl.pallas_call(functools.partial(gather_kernel, n_wide, n_grp, cap), out_...  36.3 us
    unnamed x1, local copies, waits for them, and re-layouts  1.24 us

profile of v3, /device:TPU:0, one launch (start us, length us, event | category | flops | bytes accessed | tf_op | source)
XLA Modules:
  0.0 37.6 jit_solution(10314640893373882661)
XLA Ops:
  0.0 36.3 %shard_map.37 = f32[1,384]{1,0:T(1,128)} custom-call(bf16[288,1024]{1,0:T(8,128)(2,1)} %embeds_ref.1, s32[288]{0:T(512)} %bucket_ref.1, s32[4]{0:T(128)} %pairs_ref.1), custom_call_target="tpu_custom_call" | custom-call | flops 3019898880 | bytes 589824 | tf_op jit(solution)/shard_map/pallas_call | solution.py:381
  36.3 1.2 %copy.5 = f32[1,384]{1,0:T(1,128)} copy(f32[1,384]{1,0:T(1,128)} %shard_map.37) | data formatting | bytes 3072

commit v4 on v3

--- a/solution.py
+++ b/solution.py
@@ -120,7 +120,7 @@
 def gather_kernel(
     n_wide, n_grp, cap, embeds_ref, bucket_ref, pairs_ref, out_ref,
     rows, bucket_row, entries, outgoing, panel, sums, result,
-    load_sem, send_sem, recv_sem, give_sem, take_sem,
+    load_sem, send_sem, pass_sem, recv_sem, give_sem, take_sem,
 ):
     me_wide, me_grp = lax.axis_index("wide"), lax.axis_index("grp")
     parity = lax.rem(me_wide, 2)
@@ -147,17 +147,19 @@
     load_pairs.start()
     barrier = pltpu.get_barrier_semaphore()
 
+    for step in range(1, n_wide):
+        pl.semaphore_signal(
+            barrier, inc=1, device_id=(lax.rem(me_wide + step, n_wide), me_grp),
+            device_id_type=MESH,
+        )
+
     @pl.when(is_home)
     def _():
-        def greet(step, carry):
-            other = lax.rem(me_wide * n_grp + me_grp + step, devices)
+        for step in range(1, n_grp):
             pl.semaphore_signal(
-                barrier, inc=1, device_id=(other // n_grp, lax.rem(other, n_grp)),
+                barrier, inc=1, device_id=(me_wide, lax.rem(me_grp + step, n_grp)),
                 device_id_type=MESH,
             )
-            return carry
-
-        lax.fori_loop(1, devices, greet, 0)
 
     @pl.when(jnp.logical_not(is_home))
     def _():
@@ -211,7 +213,7 @@
             src_ref=outgoing.at[turn * half + m],
             dst_ref=panel.at[pl.ds(pl.multiple_of(place * cap, cap), cap)],
             send_sem=send_sem.at[turn * half + m], recv_sem=recv_sem.at[place],
-            device_id=(2 * m + odd, n_grp // 2 - odd), device_id_type=MESH,
+            device_id=(2 * m + odd, me_grp), device_id_type=MESH,
         )
 
     fill(0)
@@ -222,28 +224,56 @@
 
     @pl.when(jnp.logical_not(is_home))
     def _():
-        pl.semaphore_wait(barrier, n_wide)
-
-    for step in range(half):
-        piece_copy(0, step).start()
+        pl.semaphore_wait(barrier, n_wide - 1 + 1)
+
+    my_order = order_of(me_grp, parity)
+
+    def panel_slot(place):
+        return panel.at[pl.ds(pl.multiple_of(place * cap, cap), cap)]
+
+    def arrive(place):
+        pltpu.make_async_copy(panel_slot(place), panel_slot(place), recv_sem.at[place]).wait()
+
+    def pass_on(index):
+        place = my_order * n_wide + index
+        return pltpu.make_async_remote_copy(
+            src_ref=panel_slot(place), dst_ref=panel_slot(place),
+            send_sem=pass_sem.at[index], recv_sem=recv_sem.at[place],
+            device_id=(me_wide, my_home), device_id_type=MESH,
+        )
+
+    def send(turn):
+        @pl.when(odd_of[turn] == parity)
+        def _():
+            place = my_order * n_wide + parity
+            pltpu.make_async_copy(
+                outgoing.at[turn * half + me_wide // 2], panel_slot(place), recv_sem.at[place]
+            ).start()
+
+        @pl.when(odd_of[turn] != parity)
+        def _():
+            piece_copy(turn, 0).start()
+
+        for step in range(1, half):
+            piece_copy(turn, step).start()
+
+    send(0)
     fill(1)
-
-    is_end = (me_grp == 0) | (me_grp == n_grp - 1)
-
-    @pl.when(is_end)
-    def _():
-        for step in range(half):
-            piece_copy(0, step).wait_send()
-            piece_copy(1, step).start()
-
-    @pl.when(jnp.logical_not(is_end))
-    def _():
-        for step in range(1, half):
-            piece_copy(1, step).start()
-
-        @pl.when(jnp.logical_not(is_home))
-        def _():
-            piece_copy(1, 0).start()
+    send(1)
+    is_far = my_order == n_grp - 1
+
+    @pl.when(is_far)
+    def _():
+        for index in range(n_wide):
+            arrive(my_order * n_wide + index)
+        for index in range(n_wide):
+            pass_on(index).start()
+
+    @pl.when(jnp.logical_not(is_far | is_home))
+    def _():
+        for index in range(n_wide):
+            arrive(my_order * n_wide + index)
+            pass_on(index).start()
 
     def shard_order(axis):
         slot = lax.broadcasted_iota(jnp.int32, (block, block), axis)
@@ -264,18 +294,8 @@
             weight = weight + jnp.where(entries[p] == named, 1.0, 0.0)
         weights.append(weight)
 
-    def arrive(place):
-        slot = panel.at[place * cap : (place + 1) * cap]
-        pltpu.make_async_copy(slot, slot, recv_sem.at[place]).wait()
-
     @pl.when(is_home)
     def _():
-        place = order_of(me_grp, parity) * n_wide + parity
-        pltpu.make_async_copy(
-            outgoing.at[half + me_wide // 2],
-            panel.at[pl.ds(pl.multiple_of(place * cap, cap), cap)],
-            recv_sem.at[place],
-        ).start()
         pick = (
             (lax.broadcasted_iota(jnp.int32, (8, 128), 1) == 0)
             .astype(jnp.float32).astype(jnp.bfloat16)
@@ -364,14 +384,18 @@
     )
     out_ref[...] = squeezed[0:1] + squeezed[16:17] + squeezed[32:33]
 
-    for step in range(half):
-        @pl.when(jnp.logical_not(is_end))
+    for turn in range(2):
+        @pl.when(odd_of[turn] != parity)
         def _():
-            piece_copy(0, step).wait_send()
-
-        @pl.when(jnp.logical_not(is_home & (step == 0)))
-        def _():
-            piece_copy(1, step).wait_send()
+            piece_copy(turn, 0).wait_send()
+
+        for step in range(1, half):
+            piece_copy(turn, step).wait_send()
+
+    @pl.when(jnp.logical_not(is_home))
+    def _():
+        for index in range(n_wide):
+            pass_on(index).wait_send()
 
 
 def gathered(embeds, bucket, pairs):
@@ -393,6 +417,7 @@
             pltpu.VMEM((8, BLK), jnp.float32),
             pltpu.SemaphoreType.DMA((3,)),
             pltpu.SemaphoreType.DMA((n_wide,)),
+            pltpu.SemaphoreType.DMA((n_wide,)),
             pltpu.SemaphoreType.DMA((n_wide * n_grp,)),
             pltpu.SemaphoreType.DMA((n_grp,)),
             pltpu.SemaphoreType.DMA,

time: 37.7 us -> 38.7 us (1.027)
  the two profiles are of different devices: /device:TPU:0 before, /device:TPU:2 now
where the time goes in v4:
time: 38.7 us; the launch traced here: 38.5 us
  Pallas kernels  37.3 us (96%)
  local copies, waits for them, and re-layouts  1.24 us (3%)
    pallas_call x1, Pallas kernels, gathered(): pl.pallas_call(functools.partial(gather_kernel, n_wide, n_grp, cap), out_...  37.3 us
    unnamed x1, local copies, waits for them, and re-layouts  1.24 us

profile of v4, /device:TPU:2, one launch (start us, length us, event | category | flops | bytes accessed | tf_op | source)
XLA Modules:
  0.0 38.5 jit_solution(17491868563491184519)
XLA Ops:
  0.0 37.3 %shard_map.37 = f32[1,384]{1,0:T(1,128)} custom-call(bf16[288,1024]{1,0:T(8,128)(2,1)} %embeds_ref.1, s32[288]{0:T(512)} %bucket_ref.1, s32[4]{0:T(128)} %pairs_ref.1), custom_call_target="tpu_custom_call" | custom-call | flops 3019898880 | bytes 589824 | tf_op jit(solution)/shard_map/pallas_call | solution.py:405
  37.3 1.2 %copy.5 = f32[1,384]{1,0:T(1,128)} copy(f32[1,384]{1,0:T(1,128)} %shard_map.37) | data formatting | bytes 3072

commit v5 on v4

--- a/solution.py
+++ b/solution.py
@@ -119,7 +119,7 @@
 
 def gather_kernel(
     n_wide, n_grp, cap, embeds_ref, bucket_ref, pairs_ref, out_ref,
-    rows, bucket_row, entries, outgoing, panel, sums, result,
+    rows, bucket_row, entries, outgoing, panel, sums, result, own_sum, squeeze,
     load_sem, send_sem, pass_sem, recv_sem, give_sem, take_sem,
 ):
     me_wide, me_grp = lax.axis_index("wide"), lax.axis_index("grp")
@@ -264,9 +264,12 @@
 
     @pl.when(is_far)
     def _():
-        for index in range(n_wide):
+        for index in range(half):
             arrive(my_order * n_wide + index)
-        for index in range(n_wide):
+        for index in range(half):
+            pass_on(index).start()
+        for index in range(half, n_wide):
+            arrive(my_order * n_wide + index)
             pass_on(index).start()
 
     @pl.when(jnp.logical_not(is_far | is_home))
@@ -293,17 +296,43 @@
         for p in range(entries.shape[0]):
             weight = weight + jnp.where(entries[p] == named, 1.0, 0.0)
         weights.append(weight)
+    own_weight = jnp.float32(0.0)
+    for p in range(entries.shape[0]):
+        own_weight = own_weight + jnp.where(entries[p] == me_grp, 1.0, 0.0)
+
+    pick = (
+        (lax.broadcasted_iota(jnp.int32, (8, 128), 1) == 0)
+        .astype(jnp.float32).astype(jnp.bfloat16)
+    )
+
+    def lane_flags(first, count):
+        lead = panel[pl.ds(first, count), :128]
+        return rows_times_rows(pick, lead)[0:1] < 2.0
+
+    def own_part():
+        first = pl.multiple_of(my_order * block, block)
+        own = panel[pl.ds(first, block), :]
+        valid = lane_flags(first, block)
+        bias = jnp.where(own[:, 0:1].astype(jnp.float32) < 2.0, -SCALE, NEVER)
+        e = jnp.exp2(
+            rows_times_rows(own, own) * SCALE + bias + jnp.where(valid, 0.0, NEVER)
+        )
+        own_sum[0:1, :] = jnp.sum(e, axis=0, keepdims=True)
+        ahead = jnp.dot(
+            jnp.broadcast_to(valid.astype(jnp.float32), (8, block)).astype(jnp.bfloat16),
+            sooner, preferred_element_type=jnp.float32,
+        )[0:1]
+        slot_place = jnp.where(valid, ahead, -1.0).astype(jnp.int32)
+        position = lax.broadcasted_iota(jnp.int32, (block, block), 0)
+        squeeze[...] = (position == slot_place).astype(jnp.float32).astype(jnp.bfloat16)
+
+    @pl.when(jnp.logical_not(is_home))
+    def _():
+        own_part()
 
     @pl.when(is_home)
     def _():
-        pick = (
-            (lax.broadcasted_iota(jnp.int32, (8, 128), 1) == 0)
-            .astype(jnp.float32).astype(jnp.bfloat16)
-        )
         ones = jnp.ones((8, 3 * 128), jnp.bfloat16)
-
-        def lane_flags(first, count):
-            return rows_times_rows(pick, panel[first : first + count, :128])[0:1] < 2.0
 
         def fold(e, lanes):
             folded = e[:, :128]
@@ -315,6 +344,8 @@
             return rows_times_rows(ones, thirds(folded, 1))[0:1]
 
         lane_bias = []
+        for k in range(n_grp):
+            sums[k, k : k + 1, :] = jnp.zeros((1, block), jnp.float32)
         for k in range(n_grp):
             base = k * block
             step_rows = 128 if k == n_grp - 1 else block
@@ -328,7 +359,6 @@
                 left = panel[base + start : base + stop]
                 bias = jnp.where(left[:, 0:1].astype(jnp.float32) < 2.0, -SCALE, NEVER)
                 valid = lane_flags(base + start, step_rows)
-                sums[k, n_grp : n_grp + 1, start:stop] = valid.astype(jnp.float32)
                 own_bias.append(jnp.where(valid, 0.0, NEVER))
                 for b in range(k):
                     right = panel[b * block : (b + 1) * block]
@@ -339,18 +369,9 @@
                     else:
                         sums[b, k : k + 1, :] += down
                     sums[k, b : b + 1, start:stop] = row_sums(fold(e, block))
-                right = panel[base : base + stop]
-                e = jnp.exp2(
-                    rows_times_rows(left, right) * SCALE + bias
-                    + jnp.concatenate(own_bias, axis=1)
-                )
-                down = jnp.sum(e, axis=0, keepdims=True)
-                if start == 0:
-                    sums[k, k : k + 1, start:stop] = down
-                else:
-                    sums[k, k : k + 1, :start] += down[:, :start]
-                    sums[k, k : k + 1, start:stop] = down[:, start:] + row_sums(fold(e, start))
             lane_bias.append(jnp.concatenate(own_bias, axis=1))
+            if k == 0:
+                own_part()
 
         keep = pltpu.make_async_copy(sums.at[0], result, take_sem)
         keep.start()
@@ -368,19 +389,11 @@
 
     pltpu.make_async_copy(result, result, take_sem).wait()
     got = result[...]
-    flags = got[n_grp : n_grp + 1]
-    ahead = jnp.dot(
-        jnp.broadcast_to(flags, (8, block)).astype(jnp.bfloat16), sooner,
-        preferred_element_type=jnp.float32,
-    )[0:1]
-    slot_place = jnp.where(flags > 0.5, ahead, -1.0).astype(jnp.int32)
-    position = lax.broadcasted_iota(jnp.int32, (block, block), 0)
-    squeeze = (position == slot_place).astype(jnp.float32).astype(jnp.bfloat16)
-    total = jnp.zeros((1, block), jnp.float32)
+    total = own_sum[0:1, :] * own_weight
     for k in range(n_grp):
         total = total + got[k : k + 1] * weights[k]
     squeezed = rows_times_rows(
-        thirds(jnp.broadcast_to(total, (16, block)), 0), squeeze
+        thirds(jnp.broadcast_to(total, (16, block)), 0), squeeze[...]
     )
     out_ref[...] = squeezed[0:1] + squeezed[16:17] + squeezed[32:33]
 
@@ -415,6 +428,8 @@
             pltpu.VMEM((n_grp * BLK, width), jnp.bfloat16),
             pltpu.VMEM((n_grp, 8, BLK), jnp.float32),
             pltpu.VMEM((8, BLK), jnp.float32),
+            pltpu.VMEM((8, BLK), jnp.float32),
+            pltpu.VMEM((BLK, BLK), jnp.bfloat16),
             pltpu.SemaphoreType.DMA((3,)),
             pltpu.SemaphoreType.DMA((n_wide,)),
             pltpu.SemaphoreType.DMA((n_wide,)),

time: 38.7 us -> 37.1 us (0.959)
  Pallas kernels: 37.3 us -> 35.7 us
    pallas_call x1, Pallas kernels: 37.3 us -> 35.7 us  [gathered(): pl.pallas_call(functools.partial(gather_kernel, n_wide, n_grp, cap), out_...]
where the time goes in v5:
time: 37.1 us; the launch traced here: 37 us
  Pallas kernels  35.7 us (96%)
  local copies, waits for them, and re-layouts  1.24 us (3%)
    pallas_call x1, Pallas kernels, gathered(): pl.pallas_call(functools.partial(gather_kernel, n_wide, n_grp, cap), out_...  35.7 us
    unnamed x1, local copies, waits for them, and re-layouts  1.24 us

profile of v5, /device:TPU:2, one launch (start us, length us, event | category | flops | bytes accessed | tf_op | source)
XLA Modules:
  0.0 37.0 jit_solution(17774120304022800798)
XLA Ops:
  0.0 35.7 %shard_map.37 = f32[1,384]{1,0:T(1,128)} custom-call(bf16[288,1024]{1,0:T(8,128)(2,1)} %embeds_ref.1, s32[288]{0:T(512)} %bucket_ref.1, s32[4]{0:T(128)} %pairs_ref.1), custom_call_target="tpu_custom_call" | custom-call | flops 3019898880 | bytes 589824 | tf_op jit(solution)/shard_map/pallas_call | solution.py:418
  35.7 1.2 %copy.5 = f32[1,384]{1,0:T(1,128)} copy(f32[1,384]{1,0:T(1,128)} %shard_map.37) | data formatting | bytes 3072

commit v6 on v5

--- a/solution.py
+++ b/solution.py
@@ -260,19 +260,7 @@
     send(0)
     fill(1)
     send(1)
-    is_far = my_order == n_grp - 1
-
-    @pl.when(is_far)
-    def _():
-        for index in range(half):
-            arrive(my_order * n_wide + index)
-        for index in range(half):
-            pass_on(index).start()
-        for index in range(half, n_wide):
-            arrive(my_order * n_wide + index)
-            pass_on(index).start()
-
-    @pl.when(jnp.logical_not(is_far | is_home))
+    @pl.when(jnp.logical_not(is_home))
     def _():
         for index in range(n_wide):
             arrive(my_order * n_wide + index)
@@ -342,6 +330,19 @@
 
         def row_sums(folded):
             return rows_times_rows(ones, thirds(folded, 1))[0:1]
+
+        def give_copy(k):
+            return pltpu.make_async_remote_copy(
+                src_ref=sums.at[k], dst_ref=result,
+                send_sem=give_sem.at[k], recv_sem=take_sem,
+                device_id=(me_wide, grp_of(k, parity)), device_id_type=MESH,
+            )
+
+        def give(k):
+            if k == 0:
+                pltpu.make_async_copy(sums.at[0], result, take_sem).start()
+            else:
+                give_copy(k).start()
 
         lane_bias = []
         for k in range(n_grp):
@@ -369,23 +370,15 @@
                     else:
                         sums[b, k : k + 1, :] += down
                     sums[k, b : b + 1, start:stop] = row_sums(fold(e, block))
+                    if k == n_grp - 1 and stop == block:
+                        give(b)
             lane_bias.append(jnp.concatenate(own_bias, axis=1))
             if k == 0:
                 own_part()
 
-        keep = pltpu.make_async_copy(sums.at[0], result, take_sem)
-        keep.start()
-        gives = []
+        give(n_grp - 1)
         for k in range(1, n_grp):
-            give = pltpu.make_async_remote_copy(
-                src_ref=sums.at[k], dst_ref=result,
-                send_sem=give_sem.at[k], recv_sem=take_sem,
-                device_id=(me_wide, grp_of(k, parity)), device_id_type=MESH,
-            )
-            give.start()
-            gives.append(give)
-        for give in gives:
-            give.wait_send()
+            give_copy(k).wait_send()
 
     pltpu.make_async_copy(result, result, take_sem).wait()
     got = result[...]

time: 37.1 us -> 36.2 us (0.976)
  the two profiles are of different devices: /device:TPU:2 before, /device:TPU:0 now
where the time goes in v6:
time: 36.2 us; the launch traced here: 36.1 us
  Pallas kernels  34.8 us (96%)
  local copies, waits for them, and re-layouts  1.24 us (3%)
    pallas_call x1, Pallas kernels, gathered(): pl.pallas_call(functools.partial(gather_kernel, n_wide, n_grp, cap), out_...  34.8 us
    unnamed x1, local copies, waits for them, and re-layouts  1.24 us

profile of v6, /device:TPU:0, one launch (start us, length us, event | category | flops | bytes accessed | tf_op | source)
XLA Modules:
  0.0 36.1 jit_solution(9569323149262391675)
XLA Ops:
  0.0 34.8 %shard_map.37 = f32[1,384]{1,0:T(1,128)} custom-call(bf16[288,1024]{1,0:T(8,128)(2,1)} %embeds_ref.1, s32[288]{0:T(512)} %bucket_ref.1, s32[4]{0:T(128)} %pairs_ref.1), custom_call_target="tpu_custom_call" | custom-call | flops 3019898880 | bytes 589824 | tf_op jit(solution)/shard_map/pallas_call | solution.py:411
  34.8 1.2 %copy.5 = f32[1,384]{1,0:T(1,128)} copy(f32[1,384]{1,0:T(1,128)} %shard_map.37) | data formatting | bytes 3072
